TPU v7x, 32 devices: a whole 2x2x4 slice. The times are simulated.
32 devices in a mesh: groups: 2 (over y), ctg: 4 (over z), tm: 4 (over x, core).
Axes of the slice: x: 2, y: 2, z: 4, core: 2. Of those that a mesh axis runs over, the one named last changes fastest.
Arguments:
- dispatch: float32 [64, 2048], P(('groups', 'tm'), 'ctg'), parts along dimension 0, may hold values from 0 to 1
- unit_cost: float32 [64, 2048], P(('groups', 'tm'), 'ctg'), parts along dimension 0, may hold values from 0.2 to 2
- capacity: float32 [2048], P('ctg'), may hold values from 0.5 to 2
- demand: float32 [64], P(('groups', 'tm')), parts along dimension 0, may hold values from 819.2 to 1228.8
- balance_dual: float32 [64], P(('groups', 'tm')), parts along dimension 0, may hold values from -6 to 6
- ramp_dual: float32 [64, 2048], P(('groups', 'tm'), 'ctg'), parts along dimension 0, may hold values from -6 to 6
- ramp_band: int32 [2048], P('ctg'), may hold values from 1 to 8
- horizon_start: int32 [32], P('tm'), may hold values 0 or 1
- shift_factors: float32 [4096, 2048], P('ctg'), may hold values from -0.125 to 0.125
- outage_factors: float32 [32, 4096], P('ctg'), may hold values from -1 to 1
- outage_line: int32 [32], P('ctg'), may hold values from 0 to 4095
- line_limit: float32 [4096], replicated, may hold values from 0.3 to 3
- flow_dual: float32 [32, 64, 4096], P('ctg', ('groups', 'tm')), parts along dimension 1, may hold values from -1 to 1
- step_sizes: float32 [4], replicated, may hold values from 0.5 to 2
Outputs:
- new_dispatch: float32 [64, 2048], P(('groups', 'tm'), 'ctg'), parts along dimension 0
- new_flow_dual: float32 [32, 64, 4096], P('ctg', ('groups', 'tm')), parts along dimension 1
- new_balance_dual: float32 [64], P(('groups', 'tm')), parts along dimension 0
- new_ramp_dual: float32 [64, 2048], P(('groups', 'tm'), 'ctg'), parts along dimension 0
There are 2 independent parts, one for each index of `groups`. A program takes and returns all parts, laid end to end along the dimension named above; an argument that names none is the same for every part. Nothing has to cross between parts.
All inputs are finite; a program needn't handle non-finite values. No bound on the sum of `horizon_start` on one device may be relied on, other than what follows from the above.
Results may differ from a plain program's by a relative error of at most 0.0003.
Values sent between devices are 32-bit elements; how exact they have to be, the bound alone decides.
A program may use at most 64 MiB of HBM per device.

v0:
```python
import jax
import jax.numpy as jnp
from jax import lax
from jax.sharding import PartitionSpec as P

BUSES = 2048


highest = lax.Precision.HIGHEST


def from_behind(block, axis, distance):
    devices = range(lax.axis_size(axis))
    route = [(i - distance, i) for i in devices if i - distance in devices]
    return lax.ppermute(block, axis, route)


def dual_update(value, step, bound):
    return value - step * jnp.clip(value / step, -bound, bound)


def local(
    dispatch,
    unit_cost,
    capacity,
    demand,
    balance_dual,
    ramp_dual,
    ramp_band,
    horizon_start,
    shift_factors,
    outage_factors,
    outage_line,
    line_limit,
    flow_dual,
    step_sizes,
):
    count_times = dispatch.shape[0]
    total_lines = outage_factors.shape[1]
    primal_step = 0.1 * step_sizes[0]
    flow_step = step_sizes[1]
    balance_step = step_sizes[2] / BUSES
    ramp_step = step_sizes[3]
    first_time = lax.axis_index("tm") * count_times
    times = first_time + jnp.arange(count_times, dtype=jnp.int32)
    coupled = jnp.where((times > 0) & (horizon_start == 0), 1.0, 0.0).astype(jnp.float32)
    ramp_limit = 0.05 * ramp_band.astype(jnp.float32)
    positions = jnp.arange(total_lines, dtype=jnp.int32)
    is_outage = positions[None, :] == outage_line[:, None]
    column = jnp.where(is_outage, -1.0, outage_factors)
    marker = is_outage.astype(jnp.float32)
    product = jnp.einsum("ctl,cl->ct", flow_dual, column, precision=highest)
    adjoint = jnp.sum(flow_dual, 0) + jnp.einsum("ct,cl->tl", product, marker, precision=highest)
    line_part = lax.psum_scatter(adjoint, "ctg", scatter_dimension=1, tiled=True)
    partial_bus = jnp.dot(line_part, shift_factors, precision=highest)
    bus_part = lax.psum_scatter(partial_bus, "ctg", scatter_dimension=1, tiled=True)
    weighted = ramp_dual * coupled[:, None]
    incoming = from_behind(weighted[:1], "tm", -1)
    following = jnp.concatenate([weighted[1:], incoming], 0)
    gradient = unit_cost + balance_dual[:, None] + bus_part + weighted - following
    new_dispatch = jnp.clip(dispatch - primal_step * gradient, 0.0, capacity[None, :])
    extended = 2.0 * new_dispatch - dispatch
    base_mine = jnp.dot(
        lax.all_gather(extended, "ctg", axis=1, tiled=True), shift_factors.T, precision=highest
    )
    total = lax.psum(jnp.sum(extended, 1), "ctg")
    base = lax.all_gather(base_mine, "ctg", axis=1, tiled=True)
    outflow = jnp.einsum("tl,cl->ct", base, marker, precision=highest)
    flow = base[None, :, :] + column[:, None, :] * outflow[:, :, None]
    new_flow_dual = dual_update(flow_dual + flow_step * flow, flow_step, line_limit[None, None, :])
    new_balance_dual = balance_dual + balance_step * (total - demand)
    previous = from_behind(extended[-1:], "tm", 1)
    before = jnp.concatenate([previous, extended[:-1]], 0)
    ramp_value = ramp_dual + ramp_step * (extended - before)
    new_ramp_dual = coupled[:, None] * dual_update(ramp_value, ramp_step, ramp_limit[None, :])
    return (new_dispatch, new_flow_dual, new_balance_dual, new_ramp_dual)


def solution(mesh):
    in_specs = (
        P(("groups", "tm"), "ctg"),
        P(("groups", "tm"), "ctg"),
        P("ctg"),
        P(("groups", "tm")),
        P(("groups", "tm")),
        P(("groups", "tm"), "ctg"),
        P("ctg"),
        P("tm"),
        P("ctg", None),
        P("ctg", None),
        P("ctg"),
        P(),
        P("ctg", ("groups", "tm"), None),
        P(),
    )
    out_specs = (
        P(("groups", "tm"), "ctg"),
        P("ctg", ("groups", "tm"), None),
        P(("groups", "tm")),
        P(("groups", "tm"), "ctg"),
    )
    return jax.shard_map(local, mesh=mesh, in_specs=in_specs, out_specs=out_specs, check_vma=False)
```

profile of v0, /device:TPU:0, one launch (start us, length us, event | category | flops | bytes accessed | tf_op | source)
XLA Modules:
  0.0 124.2 jit_solution(9553588375314222472)
XLA Ops:
  7.2 0.0 copy-start.1
  7.2 0.0 reduce-scatter.3.cloned.1.call-start
  7.3 0.7 and_select_fusion
  8.0 0.8 broadcast_multiply_fusion
  8.8 1.3 %collective-permute-start = (f32[1,512]{1,0:T(1,128)S(1)}, f32[1,512]{1,0:T(1,128)S(1)}, u32[]{:S(2)}, u32[]{:S(2)}) collective-permute-start(f32[1,512]{1,0:T(1,128)S(1)} %slice.33), channel_id=1, source_target_pairs={{1,0},{2,1},{3,2},{5,4},{6,5},{7,6},{9,8},{10,9},{11,10},{13,12},{... | collective-permute-start | bytes 6152 | tf_op jit(solution)/shard_map/ppermute | solution.py:15
  10.1 1.0 fusion.25
  11.1 3.4 %fusion = f32[8,1,8]{2,1,0:T(1,128)S(1)} fusion(f32[8,8,4096]{2,1,0:T(8,128)} %param.26, f32[8,4096,1]{1,0,2:T(8,128)S(1)} %fusion.25), kind=kOutput, calls=%fused_computation.2 | convolution fusion | flops 3145728 | bytes 1179904 | tf_op jit(solution)/shard_map/ctl,cl->ct/dot_general | solution.py:52
  14.5 1.3 %reduce_sum.18 = f32[8,4096]{1,0:T(8,128)S(1)} reduce(f32[8,8,4096]{2,1,0:T(8,128)} %param.26, f32[]{:T(128)} %constant.10.clone.1), dimensions={0}, to_apply=%region_0.1 | reduce | flops 229376 | bytes 1179652 | tf_op jit(solution)/shard_map/reduce_sum | solution.py:53
  15.8 1.6 %convolution_add_fusion = f32[8,4096]{1,0:T(8,128)} fusion(f32[8,4096]{1,0:T(8,128)S(1)} %reduce_sum.18, f32[8,8]{1,0:T(8,128)S(1)} %bitcast.17, s32[8]{0:T(128)} %param.24), kind=kOutput, calls=%fused_computation | convolution fusion | flops 3211264 | bytes 262432 | tf_op jit(solution)/shard_map/ct,cl->tl/dot_general | solution.py:53
  17.4 0.0 reduce-scatter.3.cloned.1.call-update
  17.4 0.0 reduce-scatter.5.cloned.1.call-start
  17.5 1.0 fusion.3
  18.5 0.0 copy-start.5
  18.5 0.0 copy-start
  18.5 0.0 copy-start.10
  18.5 21.7 %reduce-scatter.3.cloned.1.call-done = f32[8,1024]{1,0:T(8,128)} async-done(((f32[8,4096]{1,0:T(8,128)}), f32[8,1024]{1,0:T(8,128)}) %reduce-scatter.3.cloned.1.call-update) | async-done | bytes 32784 | tf_op jit(solution)/shard_map/reduce_scatter | solution.py:54
  40.2 8.1 %fusion.16 = f32[8,2048]{1,0:T(8,128)} fusion(f32[8,1024]{1,0:T(8,128)} %reduce-scatter.3.cloned.1.call-done, f32[1024,2048]{1,0:T(8,128)} %param.22), kind=kOutput, calls=%fused_computation.26 | convolution fusion | flops 201326592 | bytes 8486912 | tf_op jit(solution)/shard_map/dot_general | solution.py:55
  48.3 0.0 reduce-scatter.5.cloned.1.call-update
  48.4 0.7 fusion.15
  50.3 0.0 collective-permute-done
  50.4 15.3 %reduce-scatter.5.cloned.1.call-done = f32[8,512]{1,0:T(8,128)} async-done(((f32[8,2048]{1,0:T(8,128)}), f32[8,512]{1,0:T(8,128)}) %reduce-scatter.5.cloned.1.call-update) | async-done | bytes 16400 | tf_op jit(solution)/shard_map/reduce_scatter | solution.py:56
  65.7 1.5 %fusion.13 = (f32[8]{0:T(128)S(1)}, f32[8,512]{1,0:T(8,128)S(1)}, f32[8,512]{1,0:T(8,128)}) fusion(f32[8,512]{1,0:T(8,128)S(1)} %copy-done.3, f32[1,512]{1,0:T(1,128)S(1)} %collective-permute-done, f32[7,512]{1,0:T(8,128)S(1)} %slice.32, f32[8,512]{1,0:T(8,128)} %reduce-scatter.5.cloned.1.call-done, f32[8,512]{1,0:T(8,128)S(1)} %copy-done.4, ...), kind=kLoop, calls=%fused_computation.24 | loop fusion | flops 53240 | bytes 116836 | tf_op jit(solution)/shard_map/reduce_sum | solution.py:66
  67.2 13.1 %all_gather.6 = f32[8,2048]{1,0:T(8,128)S(1)} all-gather(f32[8,512]{1,0:T(8,128)S(1)} %get-tuple-element.5), channel_id=1, replica_groups=mesh['groups'=2,'ctg'=4,'tm'=4] {'ctg'}, dimensions={1}, use_global_device_ids=true | all-gather | bytes 81920 | tf_op jit(solution)/shard_map/all_gather | solution.py:64
  80.4 8.9 %psum.7 = f32[8]{0:T(128)S(1)} all-reduce(f32[8]{0:T(128)S(1)} %get-tuple-element.4), channel_id=1, replica_groups=mesh['groups'=2,'ctg'=4,'tm'=4] {'ctg'}, use_global_device_ids=true, to_apply=%region_4.5 | all-reduce | flops 8 | bytes 64 | tf_op jit(solution)/shard_map/psum | solution.py:66
  89.3 1.3 %collective-permute-start.1 = (f32[1,512]{1,0:T(1,128)S(1)}, f32[1,512]{1,0:T(1,128)S(1)}, u32[]{:S(2)}, u32[]{:S(2)}) collective-permute-start(f32[1,512]{1,0:T(1,128)S(1)} %slice.34), channel_id=1, source_target_pairs={{0,1},{1,2},{2,3},{4,5},{5,6},{6,7},{8,9},{9,10},{10,11},{12,13},{... | collective-permute-start | bytes 6152 | tf_op jit(solution)/shard_map/ppermute | solution.py:15
  90.5 9.2 %fusion.17 = f32[8,1024]{1,0:T(8,128)S(1)} fusion(f32[8,2048]{1,0:T(8,128)S(1)} %all_gather.6, f32[1024,2048]{1,0:T(8,128)} %param.22), kind=kOutput, calls=%fused_computation.27 | convolution fusion | flops 201326592 | bytes 8486912 | tf_op jit(solution)/shard_map/dot_general | solution.py:63
  99.7 13.4 %all_gather.7 = f32[8,4096]{1,0:T(8,128)S(1)} all-gather(f32[8,1024]{1,0:T(8,128)S(1)} %fusion.17), channel_id=1, replica_groups=mesh['groups'=2,'ctg'=4,'tm'=4] {'ctg'}, dimensions={1}, use_global_device_ids=true | all-gather | bytes 163840 | tf_op jit(solution)/shard_map/all_gather | solution.py:67
  113.1 0.3 fusion.2
  113.4 2.0 %multiply_subtract_fusion = f32[8,8,4096]{2,1,0:T(8,128)} fusion(f32[8,8,4096]{2,1,0:T(8,128)S(1)} %copy-done, f32[4096]{0:T(1024)S(1)} %neg.8, f32[4096]{0:T(1024)S(1)} %copy-done.2, f32[8,8]{1,0:T(8,128)S(1)} %fusion.2, f32[8,4096]{1,0:T(8,128)S(1)} %fusion.3, f32[8,4096]{1,0:T(8,128)S(1)} %all_gather.7, f32[]{:T(128)} %bitcast.4), kind=kLoop, calls=%fused_computation.1 | loop fusion | flops 2359296 | bytes 2392324 | tf_op jit(solution)/shard_map/sub | solution.py:19
  115.5 0.5 multiply_add_fusion
  116.0 0.0 collective-permute-done.1
  116.0 1.4 %subtract_multiply_fusion = f32[8,512]{1,0:T(8,128)} fusion(f32[8,512]{1,0:T(8,128)S(1)} %copy-done.1, f32[8,512]{1,0:T(8,128)S(1)} %get-tuple-element.5, f32[7,512]{1,0:T(8,128)S(1)} %bitcast.16, f32[1,512]{1,0:T(1,128)S(1)} %collective-permute-done.1, f32[512]{0:T(512)S(1)} %get-tuple-element.8, f32[512]{0:T(512)S(1)} %get-tuple-element.7, f32[]{:T(128)} %bitcast.6, ...), kind=kLoop, calls=%fused_computation.17 | loop fusion | flops 40960 | bytes 69668 | tf_op jit(solution)/shard_map/mul | solution.py:75
  (23 shorter events, 0.1 us)
Async XLA Ops:
  7.2 58.5 %copy-start.1 = (f32[8,512]{1,0:T(8,128)S(1)}, f32[8,512]{1,0:T(8,128)}, u32[]{:S(2)}) copy-start(f32[8,512]{1,0:T(8,128)} %param.19) | copy-start | bytes 49156
  7.2 41.2 %copy-start.9 = (s32[512]{0:T(512)S(1)}, s32[512]{0:T(512)}, u32[]{:S(2)}) copy-start(s32[512]{0:T(512)} %param.20) | copy-start | bytes 6148
  7.2 41.2 %copy-start.6 = (f32[4]{0:T(128)S(1)}, f32[4]{0:T(128)}, u32[]{:S(2)}) copy-start(f32[4]{0:T(128)} %param.27) | copy-start | bytes 52
  7.2 41.8 %copy-start.2 = (f32[4096]{0:T(1024)S(1)}, f32[4096]{0:T(1024)}, u32[]{:S(2)}) copy-start(f32[4096]{0:T(1024)} %param.25) | copy-start | bytes 49156
  7.2 58.5 %copy-start.8 = (f32[8]{0:T(128)S(1)}, f32[8]{0:T(128)}, u32[]{:S(2)}) copy-start(f32[8]{0:T(128)} %param.18) | copy-start | bytes 100
  7.2 58.5 %copy-start.7 = (f32[512]{0:T(512)S(1)}, f32[512]{0:T(512)}, u32[]{:S(2)}) copy-start(f32[512]{0:T(512)} %param.16) | copy-start | bytes 6148
  7.2 58.5 %copy-start.4 = (f32[8,512]{1,0:T(8,128)S(1)}, f32[8,512]{1,0:T(8,128)}, u32[]{:S(2)}) copy-start(f32[8,512]{1,0:T(8,128)} %param.15) | copy-start | bytes 49156
  7.2 58.5 %copy-start.3 = (f32[8,512]{1,0:T(8,128)S(1)}, f32[8,512]{1,0:T(8,128)}, u32[]{:S(2)}) copy-start(f32[8,512]{1,0:T(8,128)} %param.14) | copy-start | bytes 49156
  7.2 33.0 %reduce-scatter.3.cloned.1.call-start = ((), (), s32[]{:S(2)}) async-start(), calls=%async_computation.2 | async-start | bytes 163840 | tf_op jit(solution)/shard_map/reduce_scatter | solution.py:54
  8.8 41.5 %collective-permute-start = (f32[1,512]{1,0:T(1,128)S(1)}, f32[1,512]{1,0:T(1,128)S(1)}, u32[]{:S(2)}, u32[]{:S(2)}) collective-permute-start(f32[1,512]{1,0:T(1,128)S(1)} %slice.33), channel_id=1, source_target_pairs={{1,0},{2,1},{3,2},{5,4},{6,5},{7,6},{9,8},{10,9},{11,10},{13,12},{... | collective-permute-start | bytes 6152 | tf_op jit(solution)/shard_map/ppermute | solution.py:15
  17.4 48.2 %reduce-scatter.5.cloned.1.call-start = ((), (), s32[]{:S(2)}) async-start(), calls=%async_computation.3 | async-start | bytes 81920 | tf_op jit(solution)/shard_map/reduce_scatter | solution.py:56
  18.5 94.6 %copy-start.5 = (s32[8]{0:T(128)S(1)}, s32[8]{0:T(128)}, u32[]{:S(2)}) copy-start(s32[8]{0:T(128)} %param.24) | copy-start | bytes 100
  18.5 94.9 %copy-start = (f32[8,8,4096]{2,1,0:T(8,128)S(1)}, f32[8,8,4096]{2,1,0:T(8,128)}, u32[]{:S(2)}) copy-start(f32[8,8,4096]{2,1,0:T(8,128)} %param.26) | copy-start | bytes 3145732
  18.5 96.9 %copy-start.10 = (f32[8]{0:T(128)S(1)}, f32[8]{0:T(128)}, u32[]{:S(2)}) copy-start(f32[8]{0:T(128)} %param.17) | copy-start | bytes 100
  89.3 26.7 %collective-permute-start.1 = (f32[1,512]{1,0:T(1,128)S(1)}, f32[1,512]{1,0:T(1,128)S(1)}, u32[]{:S(2)}, u32[]{:S(2)}) collective-permute-start(f32[1,512]{1,0:T(1,128)S(1)} %slice.34), channel_id=1, source_target_pairs={{0,1},{1,2},{2,3},{4,5},{5,6},{6,7},{8,9},{9,10},{10,11},{12,13},{... | collective-permute-start | bytes 6152 | tf_op jit(solution)/shard_map/ppermute | solution.py:15
Sparse Core Ops, SparseCore 0:
  17.6 22.6 reduce-scatter.2
  48.4 17.1 reduce-scatter.4
where the time goes:
time: 125 us; the launch traced here: 124 us
  waiting for transfers between devices  37.1 us (30%)
  blocking collectives  35.4 us (28%)
  matrix products  22.6 us (18%)
  between operations  15.5 us (12%)
  other arithmetic  10.2 us (8%)
  starting transfers between devices  2.64 us (2%)
    reduce_scatter x1, waiting for transfers between devices, local(): lax.psum_scatter(adjoint, 'ctg', scatter_dimension=1, tiled=True)  21.7 us
    reduce_scatter x1, waiting for transfers between devices, local(): lax.psum_scatter(partial_bus, 'ctg', scatter_dimension=1, tiled=True)  15.3 us
    all_gather x1, blocking collectives, local(): base = lax.all_gather(base_mine, 'ctg', axis=1, tiled=True)  13.4 us
    all_gather x1, blocking collectives, local(): lax.all_gather(extended, 'ctg', axis=1, tiled=True)  13.1 us
    dot_general x1, matrix products, local(): jnp.dot(lax.all_gather(extended, 'ctg', axis=1, tiled=True), shift_factor...  9.19 us
    psum x1, blocking collectives, local(): total = lax.psum(jnp.sum(extended, 1), 'ctg')  8.89 us
    dot_general x1, matrix products, local(): partial_bus = jnp.dot(line_part, shift_factors, precision=highest)  8.06 us
    dot_general x1, matrix products, local(): product = jnp.einsum('ctl,cl->ct', flow_dual, column, precision=highest)  3.44 us
  transfers between devices with their start and end apart: 4, of which 2 were waited for; matrix products, arithmetic and copies ran while one was open for 23% of the time, Pallas kernels for 0%

commit v1 on v0

--- a/solution.py
+++ b/solution.py
@@ -1,6 +1,9 @@
+import functools
 import jax
 import jax.numpy as jnp
 from jax import lax
+from jax.experimental import pallas as pl
+from jax.experimental.pallas import tpu as pltpu
 from jax.sharding import PartitionSpec as P
 
 BUSES = 2048
@@ -76,6 +79,411 @@
     return (new_dispatch, new_flow_dual, new_balance_dual, new_ramp_dual)
 
 
+MESH = pl.DeviceIdType.MESH
+LANES = 128
+
+
+def partner(me, k):
+    if k == 3:
+        return 3 - me
+    if k == 2:
+        return lax.rem(me + 2, 4)
+    return me + 1 - 2 * lax.rem(me, 2)
+
+
+def column_of(scalars, rows, dtype):
+    place = lax.broadcasted_iota(jnp.int32, (rows, 1), 0)
+    result = jnp.zeros((rows, 1), dtype)
+    for i in range(rows):
+        result = jnp.where(place == i, scalars[i], result)
+    return result
+
+
+def split(x):
+    high = x.astype(jnp.bfloat16)
+    low = (x - high.astype(jnp.float32)).astype(jnp.bfloat16)
+    return high, low
+
+
+def times(x, high, low, axis):
+    rows = x.shape[0]
+    both = jnp.concatenate(split(x), 0)
+    dims = (((1,), (axis,)), ((), ()))
+    a = lax.dot_general(both, high, dims, preferred_element_type=jnp.float32)
+    b = lax.dot_general(both, low, dims, preferred_element_type=jnp.float32)
+    c = a + b
+    return c[:rows] + c[rows:]
+
+
+def kernel(
+    buses,
+    demand,
+    balance_dual,
+    horizon_start,
+    outage_line,
+    step_sizes,
+    dispatch_in,
+    unit_cost_in,
+    capacity_in,
+    ramp_dual_in,
+    ramp_band_in,
+    shift_in,
+    outage_in,
+    limit_in,
+    flow_in,
+    new_dispatch,
+    new_flow,
+    new_balance,
+    new_ramp,
+    dispatch,
+    unit_cost,
+    capacity,
+    ramp_dual,
+    ramp_band,
+    shift,
+    column,
+    limit,
+    flow,
+    high,
+    low,
+    adjoint,
+    adjoint_got,
+    bus,
+    bus_got,
+    extended_all,
+    base_all,
+    row_out,
+    row_in,
+    last_out,
+    last_in,
+    load_sem,
+    shift_sem,
+    send_sem,
+    recv_sem,
+    row_send,
+    row_recv,
+):
+    me = lax.axis_index("ctg")
+    tm = lax.axis_index("tm")
+    tms = lax.axis_size("tm")
+    ctgs, rows, lines = flow.shape
+    mine_lines = lines // 4
+    mine_buses = buses // 4
+    f32 = jnp.float32
+    after = lax.rem(tm + 1, tms)
+    ahead = lax.rem(tm + tms - 1, tms)
+
+    loads = [
+        pltpu.make_async_copy(a, b, load_sem.at[i])
+        for i, (a, b) in enumerate(
+            [
+                (flow_in, flow),
+                (outage_in, column),
+                (ramp_dual_in, ramp_dual),
+                (dispatch_in, dispatch),
+                (unit_cost_in, unit_cost),
+                (capacity_in, capacity),
+                (ramp_band_in, ramp_band),
+                (limit_in, limit),
+            ]
+        )
+    ]
+    for load in loads:
+        load.start()
+    pieces = shift_sem.shape[0]
+    depth = mine_lines // pieces
+
+    def piece(i):
+        there = pl.ds(pl.multiple_of(i * depth, depth), depth)
+        return pltpu.make_async_copy(shift_in.at[there], shift.at[there], shift_sem.at[i])
+
+    for i in range(pieces):
+        piece(i).start()
+
+    barrier = pltpu.get_barrier_semaphore()
+    for k in (3, 2, 1):
+        pl.semaphore_signal(barrier, inc=1, device_id={"ctg": partner(me, k)}, device_id_type=MESH)
+    for t in (after, ahead):
+        pl.semaphore_signal(barrier, inc=1, device_id={"tm": t}, device_id_type=MESH)
+
+    primal_step = 0.1 * step_sizes[0]
+    flow_step = step_sizes[1]
+    balance_step = step_sizes[2] / buses
+    ramp_step = step_sizes[3]
+    starts = column_of(horizon_start, rows, jnp.int32)
+    time = tm * rows + lax.broadcasted_iota(jnp.int32, (rows, 1), 0)
+    coupled = jnp.where((time > 0) & (starts == 0), 1.0, 0.0).astype(f32)
+    balance = column_of(balance_dual, rows, f32)
+    lane = lax.broadcasted_iota(jnp.int32, (rows, LANES), 1)
+    line_of = column_of(outage_line, ctgs, jnp.int32)
+
+    loads[1].wait()
+    position = lax.broadcasted_iota(jnp.int32, (ctgs, lines), 1)
+    column[...] = jnp.where(position == line_of, -1.0, column[...])
+    loads[0].wait()
+
+    def gather_product(k, sums):
+        here = pl.ds(pl.multiple_of(k * LANES, LANES), LANES)
+        total = jnp.zeros((rows, LANES), f32)
+        result = []
+        for c in range(ctgs):
+            duals = flow[c, :, here]
+            total = total + duals
+            result.append(sums[c] + duals * column[c : c + 1, here])
+        adjoint[:, here] = total
+        return tuple(result)
+
+    zeros = tuple(jnp.zeros((rows, LANES), f32) for c in range(ctgs))
+    sums = lax.fori_loop(0, lines // LANES, gather_product, zeros, unroll=4)
+    product = [jnp.sum(s, 1, keepdims=True) for s in sums]
+
+    def add_product(k, unused):
+        here = pl.ds(pl.multiple_of(k * LANES, LANES), LANES)
+        total = adjoint[:, here]
+        for c in range(ctgs):
+            total = total + jnp.where(lane == outage_line[c] - k * LANES, product[c], 0.0)
+        adjoint[:, here] = total
+        return unused
+
+    lax.fori_loop(0, lines // LANES, add_product, 0, unroll=4)
+
+    def to_partner(phase, k, source, target):
+        return pltpu.make_async_remote_copy(
+            src_ref=source,
+            dst_ref=target,
+            send_sem=send_sem.at[phase, k - 1],
+            recv_sem=recv_sem.at[phase, k - 1],
+            device_id={"ctg": partner(me, k)},
+            device_id_type=MESH,
+        )
+
+    def span(i, width):
+        return pl.ds(pl.multiple_of(i * width, width), width)
+
+    pl.semaphore_wait(barrier, 5)
+    first = {}
+    for k in (3, 2, 1):
+        first[k] = to_partner(0, k, adjoint.at[:, span(partner(me, k), mine_lines)], adjoint_got.at[k - 1])
+        first[k].start()
+    loads[2].wait()
+    weighted = ramp_dual[...] * coupled
+    row_out[...] = weighted[:1]
+    row_copy = pltpu.make_async_remote_copy(
+        src_ref=row_out, dst_ref=row_in, send_sem=row_send.at[0], recv_sem=row_recv.at[0],
+        device_id={"tm": ahead}, device_id_type=MESH)
+    row_copy.start()
+
+    @pl.loop(0, pieces)
+    def _(i):
+        piece(i).wait()
+
+        @pl.loop(0, depth // 16)
+        def _(r):
+            there = pl.ds(pl.multiple_of(i * depth + r * 16, 16), 16)
+            a, b = split(shift[there])
+            high[there] = a
+            low[there] = b
+
+    for load in loads[3:]:
+        load.wait()
+
+    line_part = adjoint[:, span(me, mine_lines)]
+    for k in (1, 2, 3):
+        first[k].wait_recv()
+        line_part = line_part + adjoint_got[k - 1]
+
+    second = {}
+    for k in (3, 2, 1, 0):
+        owner = partner(me, k) if k else me
+        there = span(owner, mine_buses)
+        part = times(line_part, high[:, there], low[:, there], 0)
+        if k:
+            bus[k - 1] = part
+            second[k] = to_partner(1, k, bus.at[k - 1], bus_got.at[k - 1])
+            second[k].start()
+    bus_part = part
+    row_copy.wait_recv()
+    sub = lax.broadcasted_iota(jnp.int32, (rows, mine_buses), 0)
+    incoming = jnp.where(tm == tms - 1, 0.0, row_in[...])
+    following = jnp.where(sub == rows - 1, incoming, jnp.roll(weighted, -1, 0))
+    known = unit_cost[...] + balance + weighted - following
+    for k in (1, 2, 3):
+        second[k].wait_recv()
+        bus_part = bus_part + bus_got[k - 1]
+    gradient = known + bus_part
+    fresh = jnp.minimum(jnp.maximum(dispatch[...] - primal_step * gradient, 0.0), capacity[...])
+    extended = 2.0 * fresh - dispatch[...]
+    extended_all[me] = extended
+    third = {}
+    for k in (3, 2, 1):
+        third[k] = to_partner(2, k, extended_all.at[me], extended_all.at[me])
+        third[k].start()
+    last_out[...] = extended[rows - 1 :]
+    last_copy = pltpu.make_async_remote_copy(
+        src_ref=last_out, dst_ref=last_in, send_sem=row_send.at[1], recv_sem=row_recv.at[1],
+        device_id={"tm": after}, device_id_type=MESH)
+    last_copy.start()
+    new_dispatch[...] = fresh
+
+    total = jnp.sum(extended, 1, keepdims=True)
+    base = None
+    for k in (0, 1, 2, 3):
+        if k:
+            third[k].wait_recv()
+        owner = partner(me, k) if k else me
+        block = extended_all[owner]
+        there = span(owner, mine_buses)
+        if k:
+            total = total + jnp.sum(block, 1, keepdims=True)
+        part = times(block, high[:, there], low[:, there], 1)
+        base = part if base is None else base + part
+    base_all[me] = base
+    fourth = {}
+    for k in (3, 2, 1):
+        fourth[k] = to_partner(3, k, base_all.at[me], base_all.at[me])
+        fourth[k].start()
+
+    wanted = column_of(demand, rows, f32)
+    settled = balance + balance_step * (total - wanted)
+    eye = lax.broadcasted_iota(jnp.int32, (rows, rows), 0) == lax.broadcasted_iota(jnp.int32, (rows, rows), 1)
+    new_balance[...] = jnp.sum(jnp.where(eye, settled, 0.0), 0, keepdims=True)
+    last_copy.wait_recv()
+    previous = jnp.where(tm == 0, 0.0, last_in[...])
+    before = jnp.where(sub == 0, previous, jnp.roll(extended, 1, 0))
+    ramp_value = ramp_dual[...] + ramp_step * (extended - before)
+    band = ramp_step * (0.05 * ramp_band[...].astype(f32))
+    new_ramp[...] = coupled * (ramp_value - jnp.minimum(jnp.maximum(ramp_value, -band), band))
+
+    for k in (1, 2, 3):
+        fourth[k].wait_recv()
+    tiles = mine_lines // LANES
+
+    def pick(k, found):
+        j = k // tiles
+        here = pl.ds(pl.multiple_of((k - j * tiles) * LANES, LANES), LANES)
+        block = base_all[j, :, here]
+        return tuple(
+            found[c] + jnp.where(lane == outage_line[c] - k * LANES, block, 0.0) for c in range(ctgs)
+        )
+
+    found = lax.fori_loop(0, lines // LANES, pick, zeros, unroll=4)
+    outflow = [flow_step * jnp.sum(f, 1, keepdims=True) for f in found]
+
+    def update(k, unused):
+        j = k // tiles
+        here = pl.ds(pl.multiple_of(k * LANES, LANES), LANES)
+        inner = pl.ds(pl.multiple_of((k - j * tiles) * LANES, LANES), LANES)
+        shared = flow_step * base_all[j, :, inner]
+        bound = flow_step * limit[:, here]
+        for c in range(ctgs):
+            value = flow[c, :, here] + (shared + column[c : c + 1, here] * outflow[c])
+            new_flow[c, :, here] = value - jnp.minimum(jnp.maximum(value, -bound), bound)
+        return unused
+
+    lax.fori_loop(0, lines // LANES, update, 0, unroll=4)
+
+    for group in (first, second, third, fourth):
+        for k in (1, 2, 3):
+            group[k].wait_send()
+    row_copy.wait_send()
+    last_copy.wait_send()
+
+
+def fused(
+    dispatch,
+    unit_cost,
+    capacity,
+    demand,
+    balance_dual,
+    ramp_dual,
+    ramp_band,
+    horizon_start,
+    shift_factors,
+    outage_factors,
+    outage_line,
+    line_limit,
+    flow_dual,
+    step_sizes,
+):
+    f32 = jnp.float32
+    rows, own = dispatch.shape
+    ctgs, unused, lines = flow_dual.shape
+    buses = shift_factors.shape[1]
+    line_block = lines // 4
+    smem = pl.BlockSpec(memory_space=pltpu.SMEM)
+    vmem = pl.BlockSpec(memory_space=pltpu.VMEM)
+    anywhere = pl.BlockSpec(memory_space=pl.ANY)
+    hbm = pl.BlockSpec(memory_space=pltpu.HBM)
+    outs = pl.pallas_call(
+        functools.partial(kernel, buses),
+        out_shape=(
+            jax.ShapeDtypeStruct((rows, own), f32),
+            jax.ShapeDtypeStruct(flow_dual.shape, f32),
+            jax.ShapeDtypeStruct((1, rows), f32),
+            jax.ShapeDtypeStruct((rows, own), f32),
+        ),
+        in_specs=[smem] * 5 + [hbm] * 9,
+        out_specs=[vmem] * 4,
+        scratch_shapes=[
+            pltpu.VMEM((rows, own), f32),
+            pltpu.VMEM((rows, own), f32),
+            pltpu.VMEM((1, own), f32),
+            pltpu.VMEM((rows, own), f32),
+            pltpu.VMEM((1, own), jnp.int32),
+            pltpu.VMEM(shift_factors.shape, f32),
+            pltpu.VMEM(outage_factors.shape, f32),
+            pltpu.VMEM((1, lines), f32),
+            pltpu.VMEM(flow_dual.shape, f32),
+            pltpu.VMEM(shift_factors.shape, jnp.bfloat16),
+            pltpu.VMEM(shift_factors.shape, jnp.bfloat16),
+            pltpu.VMEM((rows, lines), f32),
+            pltpu.VMEM((3, rows, line_block), f32),
+            pltpu.VMEM((3, rows, own), f32),
+            pltpu.VMEM((3, rows, own), f32),
+            pltpu.VMEM((4, rows, own), f32),
+            pltpu.VMEM((4, rows, line_block), f32),
+            pltpu.VMEM((1, own), f32),
+            pltpu.VMEM((1, own), f32),
+            pltpu.VMEM((1, own), f32),
+            pltpu.VMEM((1, own), f32),
+            pltpu.SemaphoreType.DMA((8,)),
+            pltpu.SemaphoreType.DMA((8,)),
+            pltpu.SemaphoreType.DMA((4, 3)),
+            pltpu.SemaphoreType.DMA((4, 3)),
+            pltpu.SemaphoreType.DMA((2,)),
+            pltpu.SemaphoreType.DMA((2,)),
+        ],
+        compiler_params=pltpu.CompilerParams(
+            collective_id=0, has_side_effects=True, vmem_limit_bytes=40 * 2**20
+        ),
+    )(
+        demand,
+        balance_dual,
+        horizon_start,
+        outage_line,
+        step_sizes,
+        dispatch,
+        unit_cost,
+        capacity.reshape(1, own),
+        ramp_dual,
+        ramp_band.reshape(1, own),
+        shift_factors,
+        outage_factors,
+        line_limit.reshape(1, lines),
+        flow_dual,
+    )
+    return outs[0], outs[1], outs[2].reshape(rows), outs[3]
+
+
+def choose(*blocks):
+    rows, own = blocks[0].shape
+    lines = blocks[9].shape[1]
+    whole = rows == 8 and own % LANES == 0 and lines % (4 * LANES) == 0
+    if lax.axis_size("ctg") == 4 and lax.axis_size("tm") > 2 and whole:
+        return fused(*blocks)
+    return local(*blocks)
+
+
 def solution(mesh):
     in_specs = (
         P(("groups", "tm"), "ctg"),
@@ -99,4 +507,4 @@
         P(("groups", "tm")),
         P(("groups", "tm"), "ctg"),
     )
-    return jax.shard_map(local, mesh=mesh, in_specs=in_specs, out_specs=out_specs, check_vma=False)
+    return jax.shard_map(choose, mesh=mesh, in_specs=in_specs, out_specs=out_specs, check_vma=False)

time: 125 us -> 42.4 us (0.34)
  waiting for transfers between devices: 37.1 us -> 0 us
  blocking collectives: 35.4 us -> 0 us
  Pallas kernels: 0 us -> 25.5 us
  matrix products: 22.6 us -> 0 us
  local copies, waits for them, and re-layouts: 0.73 us -> 15.7 us
  between operations: 15.5 us -> 0.67 us
  other arithmetic: 10.2 us -> 0 us
  starting transfers between devices: 2.64 us -> 0 us
    reduce_scatter x2 -> x0, waiting for transfers between devices: 37 us -> none  [the longest x1 21.7 us: local(): lax.psum_scatter(adjoint, 'ctg', scatter_dimension=1, tiled=True)]
    all_gather x2 -> x0, blocking collectives: 26.5 us -> none  [the longest x1 13.4 us: local(): base = lax.all_gather(base_mine, 'ctg', axis=1, tiled=True)]
    pallas_call x0 -> x1, Pallas kernels: none -> 25.5 us  [fused(): pl.pallas_call(functools.partial(kernel, buses), out_shape=(jax.ShapeDtyp...]
    dot_general x5 -> x0, matrix products: 22.6 us -> none  [the longest x1 9.19 us: local(): jnp.dot(lax.all_gather(extended, 'ctg', axis=1, tiled=True), shift_factor...]
    unnamed x22 -> x32, local copies, waits for them, and re-layouts: 0.05 us -> 15.7 us
    psum x1 -> x0, blocking collectives: 8.89 us -> none  [local(): total = lax.psum(jnp.sum(extended, 1), 'ctg')]
    reduce_sum x2 -> x0, other arithmetic: 2.82 us -> none  [the longest x1 1.52 us: local(): total = lax.psum(jnp.sum(extended, 1), 'ctg')]
    select_n x3 -> x0, other arithmetic: 2.69 us -> none  [the longest x2 1.97 us: local(): column = jnp.where(is_outage, -1.0, outage_factors)]
  transfers between devices with their start and end apart: 4 -> 0, of which waited for: 2 -> 0; matrix products, arithmetic and copies ran while one was open for 23% -> 0% of each run, Pallas kernels for 0% -> 0%
where the time goes in v1:
time: 42.4 us; the launch traced here: 41.9 us
  Pallas kernels  25.5 us (60%)
  local copies, waits for them, and re-layouts  15.7 us (37%)
  between operations  0.67 us (2%)
    pallas_call x1, Pallas kernels, fused(): pl.pallas_call(functools.partial(kernel, buses), out_shape=(jax.ShapeDtyp...  25.5 us
    unnamed x32, local copies, waits for them, and re-layouts  15.7 us

profile of v1, /device:TPU:0, one launch (start us, length us, event | category | flops | bytes accessed | tf_op | source)
XLA Modules:
  0.0 41.9 jit_solution(14786179419562110387)
XLA Ops:
  0.6 0.0 copy-start
  0.6 3.4 %copy-done = f32[1024,2048]{1,0:T(8,128)S(1)} copy-done((f32[1024,2048]{1,0:T(8,128)S(1)}, f32[1024,2048]{1,0:T(8,128)}, u32[]{:S(2)}) %copy-start) | copy-done | bytes 8388632
  4.0 0.0 copy-start.1
  4.0 1.2 %copy-done.1 = f32[8,8,4096]{2,1,0:T(8,128)S(1)} copy-done((f32[8,8,4096]{2,1,0:T(8,128)S(1)}, f32[8,8,4096]{2,1,0:T(8,128)}, u32[]{:S(2)}) %copy-start.1) | copy-done | bytes 1048600
  5.2 0.0 copy-start.2
  5.2 0.9 %copy-done.2 = f32[8,4096]{1,0:T(8,128)S(1)} copy-done((f32[8,4096]{1,0:T(8,128)S(1)}, f32[8,4096]{1,0:T(8,128)}, u32[]{:S(2)}) %copy-start.2) | copy-done | bytes 131096
  6.1 0.0 copy-start.3
  6.2 0.7 %copy-done.3 = f32[8,512]{1,0:T(8,128)S(1)} copy-done((f32[8,512]{1,0:T(8,128)S(1)}, f32[8,512]{1,0:T(8,128)}, u32[]{:S(2)}) %copy-start.3) | copy-done | bytes 16408
  6.9 0.0 copy-start.4
  6.9 0.7 %copy-done.4 = f32[8,512]{1,0:T(8,128)S(1)} copy-done((f32[8,512]{1,0:T(8,128)S(1)}, f32[8,512]{1,0:T(8,128)}, u32[]{:S(2)}) %copy-start.4) | copy-done | bytes 16408
  7.6 0.0 copy-start.5
  7.6 0.7 %copy-done.5 = f32[8,512]{1,0:T(8,128)S(1)} copy-done((f32[8,512]{1,0:T(8,128)S(1)}, f32[8,512]{1,0:T(8,128)}, u32[]{:S(2)}) %copy-start.5) | copy-done | bytes 16408
  8.3 0.0 copy-start.6
  8.3 0.7 %copy-done.6 = f32[4096]{0:T(1024)S(1)} copy-done((f32[4096]{0:T(1024)S(1)}, f32[4096]{0:T(1024)}, u32[]{:S(2)}) %copy-start.6) | copy-done | bytes 16408
  9.0 0.0 copy-start.7
  9.0 0.7 %copy-done.7 = f32[512]{0:T(512)S(1)} copy-done((f32[512]{0:T(512)S(1)}, f32[512]{0:T(512)}, u32[]{:S(2)}) %copy-start.7) | copy-done | bytes 2072
  9.7 0.0 copy-start.8
  9.7 0.7 %copy-done.8 = s32[512]{0:T(512)S(1)} copy-done((s32[512]{0:T(512)S(1)}, s32[512]{0:T(512)}, u32[]{:S(2)}) %copy-start.8) | copy-done | bytes 2072
  10.4 0.0 copy-start.9
  10.4 0.7 %copy-done.9 = f32[8]{0:T(128)S(1)} copy-done((f32[8]{0:T(128)S(1)}, f32[8]{0:T(128)}, u32[]{:S(2)}) %copy-start.9) | copy-done | bytes 56
  11.0 0.0 copy-start.10
  11.0 0.7 %copy-done.10 = f32[8]{0:T(128)S(1)} copy-done((f32[8]{0:T(128)S(1)}, f32[8]{0:T(128)}, u32[]{:S(2)}) %copy-start.10) | copy-done | bytes 56
  11.7 0.7 %copy-done.11 = s32[8]{0:T(128)S(1)} copy-done((s32[8]{0:T(128)S(1)}, s32[8]{0:T(128)}, u32[]{:S(2)}) %copy-start.11) | copy-done | bytes 56
  12.4 0.0 copy-start.12
  12.4 0.7 %copy-done.12 = s32[8]{0:T(128)S(1)} copy-done((s32[8]{0:T(128)S(1)}, s32[8]{0:T(128)}, u32[]{:S(2)}) %copy-start.12) | copy-done | bytes 56
  13.0 0.0 copy-start.13
  13.0 0.7 %copy-done.13 = f32[4]{0:T(128)S(1)} copy-done((f32[4]{0:T(128)S(1)}, f32[4]{0:T(128)}, u32[]{:S(2)}) %copy-start.13) | copy-done | bytes 40
  13.7 25.5 %shard_map.165 = (f32[8,512]{1,0:T(8,128)S(1)}, f32[8,8,4096]{2,1,0:T(8,128)S(1)}, f32[1,8]{1,0:T(1,128)S(1)}, f32[8,512]{1,0:T(8,128)S(1)}) custom-call(f32[8]{0:T(128)S(1)} %copy-done.9, f32[8]{0:T(128)S(1)} %copy-done.10, s32[8]{0:T(128)S(1)} %copy-done.11, s32[8]{0:T(128)S(1)} %copy-done.12, f32[4]{0:T(128)S(1)} %copy-done.13, f32[8,512]{1,0:T(8,128)S(1)} %copy-done.3, ...), custom_call_target="tpu_custom_call" | custom-call | tf_op jit(solution)/shard_map/pallas_call | solution.py:417
  39.2 0.6 %copy.22 = f32[8,512]{1,0:T(8,128)} copy(f32[8,512]{1,0:T(8,128)S(1)} %get-tuple-element.16) | data formatting | bytes 32768
  39.8 1.0 %copy.23 = f32[8,8,4096]{2,1,0:T(8,128)} copy(f32[8,8,4096]{2,1,0:T(8,128)S(1)} %get-tuple-element.17) | data formatting | bytes 2097152
  40.8 0.5 %copy.24 = f32[8]{0:T(128)} copy(f32[8]{0:T(128)S(1)} %bitcast.7) | data formatting | bytes 64
  41.3 0.6 %copy.25 = f32[8,512]{1,0:T(8,128)} copy(f32[8,512]{1,0:T(8,128)S(1)} %get-tuple-element.19) | data formatting | bytes 32768
  (1 shorter events, 0.0 us)
Async XLA Ops:
  0.6 3.4 %copy-start = (f32[1024,2048]{1,0:T(8,128)S(1)}, f32[1024,2048]{1,0:T(8,128)}, u32[]{:S(2)}) copy-start(f32[1024,2048]{1,0:T(8,128)} %shift_in.1) | copy-start | bytes 25165828
  4.0 1.2 %copy-start.1 = (f32[8,8,4096]{2,1,0:T(8,128)S(1)}, f32[8,8,4096]{2,1,0:T(8,128)}, u32[]{:S(2)}) copy-start(f32[8,8,4096]{2,1,0:T(8,128)} %flow_in.1) | copy-start | bytes 3145732
  5.2 0.9 %copy-start.2 = (f32[8,4096]{1,0:T(8,128)S(1)}, f32[8,4096]{1,0:T(8,128)}, u32[]{:S(2)}) copy-start(f32[8,4096]{1,0:T(8,128)} %outage_in.1) | copy-start | bytes 393220
  6.1 0.7 %copy-start.3 = (f32[8,512]{1,0:T(8,128)S(1)}, f32[8,512]{1,0:T(8,128)}, u32[]{:S(2)}) copy-start(f32[8,512]{1,0:T(8,128)} %dispatch_in.1) | copy-start | bytes 49156
  6.9 0.7 %copy-start.4 = (f32[8,512]{1,0:T(8,128)S(1)}, f32[8,512]{1,0:T(8,128)}, u32[]{:S(2)}) copy-start(f32[8,512]{1,0:T(8,128)} %unit_cost_in.1) | copy-start | bytes 49156
  7.6 0.7 %copy-start.5 = (f32[8,512]{1,0:T(8,128)S(1)}, f32[8,512]{1,0:T(8,128)}, u32[]{:S(2)}) copy-start(f32[8,512]{1,0:T(8,128)} %ramp_dual_in.1) | copy-start | bytes 49156
  8.3 0.7 %copy-start.6 = (f32[4096]{0:T(1024)S(1)}, f32[4096]{0:T(1024)}, u32[]{:S(2)}) copy-start(f32[4096]{0:T(1024)} %param.25) | copy-start | bytes 49156
  9.0 0.7 %copy-start.7 = (f32[512]{0:T(512)S(1)}, f32[512]{0:T(512)}, u32[]{:S(2)}) copy-start(f32[512]{0:T(512)} %param.16) | copy-start | bytes 6148
  9.7 0.7 %copy-start.8 = (s32[512]{0:T(512)S(1)}, s32[512]{0:T(512)}, u32[]{:S(2)}) copy-start(s32[512]{0:T(512)} %param.20) | copy-start | bytes 6148
  10.4 0.7 %copy-start.9 = (f32[8]{0:T(128)S(1)}, f32[8]{0:T(128)}, u32[]{:S(2)}) copy-start(f32[8]{0:T(128)} %demand.1) | copy-start | bytes 100
  11.0 0.7 %copy-start.10 = (f32[8]{0:T(128)S(1)}, f32[8]{0:T(128)}, u32[]{:S(2)}) copy-start(f32[8]{0:T(128)} %balance_dual.1) | copy-start | bytes 100
  11.7 0.7 %copy-start.11 = (s32[8]{0:T(128)S(1)}, s32[8]{0:T(128)}, u32[]{:S(2)}) copy-start(s32[8]{0:T(128)} %horizon_start.1) | copy-start | bytes 100
  12.4 0.7 %copy-start.12 = (s32[8]{0:T(128)S(1)}, s32[8]{0:T(128)}, u32[]{:S(2)}) copy-start(s32[8]{0:T(128)} %outage_line.1) | copy-start | bytes 100
  13.0 0.7 %copy-start.13 = (f32[4]{0:T(128)S(1)}, f32[4]{0:T(128)}, u32[]{:S(2)}) copy-start(f32[4]{0:T(128)} %step_sizes.1) | copy-start | bytes 52

commit v2 on v1

--- a/solution.py
+++ b/solution.py
@@ -117,11 +117,11 @@
 
 def kernel(
     buses,
-    demand,
-    balance_dual,
-    horizon_start,
-    outage_line,
-    step_sizes,
+    demand_in,
+    balance_in,
+    start_in,
+    outage_line_in,
+    step_in,
     dispatch_in,
     unit_cost_in,
     capacity_in,
@@ -129,10 +129,17 @@
     ramp_band_in,
     shift_in,
     outage_in,
-    limit_in,
     flow_in,
+    dispatch_to,
+    base_to,
+    balance_to,
+    ramp_to,
+    demand,
+    balance_dual,
+    horizon_start,
+    outage_line,
+    step_sizes,
     new_dispatch,
-    new_flow,
     new_balance,
     new_ramp,
     dispatch,
@@ -142,7 +149,6 @@
     ramp_band,
     shift,
     column,
-    limit,
     flow,
     high,
     low,
@@ -157,6 +163,7 @@
     last_out,
     last_in,
     load_sem,
+    store_sem,
     shift_sem,
     send_sem,
     recv_sem,
@@ -173,6 +180,12 @@
     after = lax.rem(tm + 1, tms)
     ahead = lax.rem(tm + tms - 1, tms)
 
+    barrier = pltpu.get_barrier_semaphore()
+    for k in (3, 2, 1):
+        pl.semaphore_signal(barrier, inc=1, device_id={"ctg": partner(me, k)}, device_id_type=MESH)
+    for t in (after, ahead):
+        pl.semaphore_signal(barrier, inc=1, device_id={"tm": t}, device_id_type=MESH)
+
     loads = [
         pltpu.make_async_copy(a, b, load_sem.at[i])
         for i, (a, b) in enumerate(
@@ -184,7 +197,11 @@
                 (unit_cost_in, unit_cost),
                 (capacity_in, capacity),
                 (ramp_band_in, ramp_band),
-                (limit_in, limit),
+                (outage_line_in, outage_line),
+                (step_in, step_sizes),
+                (start_in, horizon_start),
+                (balance_in, balance_dual),
+                (demand_in, demand),
             ]
         )
     ]
@@ -200,12 +217,8 @@
     for i in range(pieces):
         piece(i).start()
 
-    barrier = pltpu.get_barrier_semaphore()
-    for k in (3, 2, 1):
-        pl.semaphore_signal(barrier, inc=1, device_id={"ctg": partner(me, k)}, device_id_type=MESH)
-    for t in (after, ahead):
-        pl.semaphore_signal(barrier, inc=1, device_id={"tm": t}, device_id_type=MESH)
-
+    for load in loads[7:]:
+        load.wait()
     primal_step = 0.1 * step_sizes[0]
     flow_step = step_sizes[1]
     balance_step = step_sizes[2] / buses
@@ -284,7 +297,7 @@
             high[there] = a
             low[there] = b
 
-    for load in loads[3:]:
+    for load in loads[3:7]:
         load.wait()
 
     line_part = adjoint[:, span(me, mine_lines)]
@@ -324,6 +337,8 @@
         device_id={"tm": after}, device_id_type=MESH)
     last_copy.start()
     new_dispatch[...] = fresh
+    stores = [pltpu.make_async_copy(new_dispatch, dispatch_to, store_sem.at[0])]
+    stores[0].start()
 
     total = jnp.sum(extended, 1, keepdims=True)
     base = None
@@ -353,40 +368,128 @@
     ramp_value = ramp_dual[...] + ramp_step * (extended - before)
     band = ramp_step * (0.05 * ramp_band[...].astype(f32))
     new_ramp[...] = coupled * (ramp_value - jnp.minimum(jnp.maximum(ramp_value, -band), band))
-
-    for k in (1, 2, 3):
-        fourth[k].wait_recv()
-    tiles = mine_lines // LANES
+    stores.append(pltpu.make_async_copy(new_balance, balance_to, store_sem.at[1]))
+    stores.append(pltpu.make_async_copy(new_ramp, ramp_to, store_sem.at[2]))
+    stores[1].start()
+    stores[2].start()
+
+    for k in (0, 1, 2, 3):
+        if k:
+            fourth[k].wait_recv()
+        owner = partner(me, k) if k else me
+        stores.append(pltpu.make_async_copy(base_all.at[owner], base_to.at[owner], store_sem.at[3 + k]))
+        stores[-1].start()
+
+    for group in (first, second, third, fourth):
+        for k in (1, 2, 3):
+            group[k].wait_send()
+    row_copy.wait_send()
+    last_copy.wait_send()
+    for store in stores:
+        store.wait()
+
+
+def finish(
+    fresh_in,
+    base_in,
+    balance_in,
+    ramp_in,
+    outage_in,
+    outage_line_in,
+    limit_in,
+    flow_in,
+    step_in,
+    fresh_to,
+    flow_to,
+    balance_to,
+    ramp_to,
+    fresh,
+    base,
+    balance,
+    ramp,
+    column,
+    outage_line,
+    limit,
+    flow,
+    step_sizes,
+    new_flow,
+    sem,
+    flow_sem,
+    store_sem,
+):
+    ctgs, rows, lines = flow.shape
+    f32 = jnp.float32
+    parts = base.shape[0]
+    width = lines // parts
+    tiles = width // LANES
+
+    def part(j):
+        return pl.ds(j * width, width)
+
+    pairs = [
+        (outage_line_in, outage_line),
+        (step_in, step_sizes),
+        (base_in, base),
+        (outage_in, column),
+        (limit_in, limit),
+        (fresh_in, fresh),
+        (balance_in, balance),
+        (ramp_in, ramp),
+    ]
+    loads = [pltpu.make_async_copy(a, b, sem.at[i]) for i, (a, b) in enumerate(pairs)]
+    flows = [
+        pltpu.make_async_copy(flow_in.at[:, :, part(j)], flow.at[:, :, part(j)], flow_sem.at[j])
+        for j in range(parts)
+    ]
+    for load in loads[:5] + flows + loads[5:]:
+        load.start()
+    for load in loads[:4]:
+        load.wait()
+    flow_step = step_sizes[1]
+    lane = lax.broadcasted_iota(jnp.int32, (rows, LANES), 1)
 
     def pick(k, found):
         j = k // tiles
         here = pl.ds(pl.multiple_of((k - j * tiles) * LANES, LANES), LANES)
-        block = base_all[j, :, here]
+        block = base[j, :, here]
         return tuple(
             found[c] + jnp.where(lane == outage_line[c] - k * LANES, block, 0.0) for c in range(ctgs)
         )
 
+    zeros = tuple(jnp.zeros((rows, LANES), f32) for c in range(ctgs))
     found = lax.fori_loop(0, lines // LANES, pick, zeros, unroll=4)
     outflow = [flow_step * jnp.sum(f, 1, keepdims=True) for f in found]
+    line_of = column_of(outage_line, ctgs, jnp.int32)
+    position = lax.broadcasted_iota(jnp.int32, (ctgs, lines), 1)
+    column[...] = jnp.where(position == line_of, -1.0, column[...])
+    for load in loads[4:]:
+        load.wait()
+    stores = [
+        pltpu.make_async_copy(a, b, store_sem.at[i])
+        for i, (a, b) in enumerate([(fresh, fresh_to), (balance, balance_to), (ramp, ramp_to)])
+    ]
+    for store in stores:
+        store.start()
 
     def update(k, unused):
         j = k // tiles
         here = pl.ds(pl.multiple_of(k * LANES, LANES), LANES)
         inner = pl.ds(pl.multiple_of((k - j * tiles) * LANES, LANES), LANES)
-        shared = flow_step * base_all[j, :, inner]
+        shared = flow_step * base[j, :, inner]
         bound = flow_step * limit[:, here]
         for c in range(ctgs):
             value = flow[c, :, here] + (shared + column[c : c + 1, here] * outflow[c])
             new_flow[c, :, here] = value - jnp.minimum(jnp.maximum(value, -bound), bound)
         return unused
 
-    lax.fori_loop(0, lines // LANES, update, 0, unroll=4)
-
-    for group in (first, second, third, fourth):
-        for k in (1, 2, 3):
-            group[k].wait_send()
-    row_copy.wait_send()
-    last_copy.wait_send()
+    for j in range(parts):
+        flows[j].wait()
+        lax.fori_loop(j * tiles, (j + 1) * tiles, update, 0, unroll=4)
+        store = pltpu.make_async_copy(new_flow.at[:, :, part(j)], flow_to.at[:, :, part(j)], store_sem.at[3 + j])
+        store.start()
+        stores.append(store)
+    for store in stores:
+        store.wait()
 
 
 def fused(
@@ -410,21 +513,24 @@
     ctgs, unused, lines = flow_dual.shape
     buses = shift_factors.shape[1]
     line_block = lines // 4
-    smem = pl.BlockSpec(memory_space=pltpu.SMEM)
-    vmem = pl.BlockSpec(memory_space=pltpu.VMEM)
     anywhere = pl.BlockSpec(memory_space=pl.ANY)
     hbm = pl.BlockSpec(memory_space=pltpu.HBM)
+    small = jax.ShapeDtypeStruct((rows, own), f32)
+    single = jax.ShapeDtypeStruct((1, rows), f32)
     outs = pl.pallas_call(
         functools.partial(kernel, buses),
-        out_shape=(
-            jax.ShapeDtypeStruct((rows, own), f32),
-            jax.ShapeDtypeStruct(flow_dual.shape, f32),
-            jax.ShapeDtypeStruct((1, rows), f32),
-            jax.ShapeDtypeStruct((rows, own), f32),
-        ),
-        in_specs=[smem] * 5 + [hbm] * 9,
-        out_specs=[vmem] * 4,
+        out_shape=(small, jax.ShapeDtypeStruct((4, rows, line_block), f32), single, small),
+        in_specs=[hbm] * 13,
+        out_specs=[anywhere] * 4,
         scratch_shapes=[
+            pltpu.SMEM((rows,), f32),
+            pltpu.SMEM((rows,), f32),
+            pltpu.SMEM((rows,), jnp.int32),
+            pltpu.SMEM((ctgs,), jnp.int32),
+            pltpu.SMEM((4,), f32),
+            pltpu.VMEM((rows, own), f32),
+            pltpu.VMEM((1, rows), f32),
+            pltpu.VMEM((rows, own), f32),
             pltpu.VMEM((rows, own), f32),
             pltpu.VMEM((rows, own), f32),
             pltpu.VMEM((1, own), f32),
@@ -432,7 +538,6 @@
             pltpu.VMEM((1, own), jnp.int32),
             pltpu.VMEM(shift_factors.shape, f32),
             pltpu.VMEM(outage_factors.shape, f32),
-            pltpu.VMEM((1, lines), f32),
             pltpu.VMEM(flow_dual.shape, f32),
             pltpu.VMEM(shift_factors.shape, jnp.bfloat16),
             pltpu.VMEM(shift_factors.shape, jnp.bfloat16),
@@ -446,7 +551,8 @@
             pltpu.VMEM((1, own), f32),
             pltpu.VMEM((1, own), f32),
             pltpu.VMEM((1, own), f32),
-            pltpu.SemaphoreType.DMA((8,)),
+            pltpu.SemaphoreType.DMA((12,)),
+            pltpu.SemaphoreType.DMA((7,)),
             pltpu.SemaphoreType.DMA((8,)),
             pltpu.SemaphoreType.DMA((4, 3)),
             pltpu.SemaphoreType.DMA((4, 3)),
@@ -454,7 +560,7 @@
             pltpu.SemaphoreType.DMA((2,)),
         ],
         compiler_params=pltpu.CompilerParams(
-            collective_id=0, has_side_effects=True, vmem_limit_bytes=40 * 2**20
+            collective_id=0, has_side_effects=True, vmem_limit_bytes=61 * 2**20
         ),
     )(
         demand,
@@ -469,9 +575,30 @@
         ramp_band.reshape(1, own),
         shift_factors,
         outage_factors,
-        line_limit.reshape(1, lines),
         flow_dual,
     )
+    outs = pl.pallas_call(
+        finish,
+        out_shape=(small, jax.ShapeDtypeStruct(flow_dual.shape, f32), single, small),
+        in_specs=[hbm] * 9,
+        out_specs=[hbm] * 4,
+        scratch_shapes=[
+            pltpu.VMEM((rows, own), f32),
+            pltpu.VMEM((4, rows, line_block), f32),
+            pltpu.VMEM((1, rows), f32),
+            pltpu.VMEM((rows, own), f32),
+            pltpu.VMEM(outage_factors.shape, f32),
+            pltpu.SMEM((ctgs,), jnp.int32),
+            pltpu.VMEM((1, lines), f32),
+            pltpu.VMEM(flow_dual.shape, f32),
+            pltpu.SMEM((4,), f32),
+            pltpu.VMEM(flow_dual.shape, f32),
+            pltpu.SemaphoreType.DMA((8,)),
+            pltpu.SemaphoreType.DMA((4,)),
+            pltpu.SemaphoreType.DMA((7,)),
+        ],
+        compiler_params=pltpu.CompilerParams(vmem_limit_bytes=61 * 2**20),
+    )(*outs, outage_factors, outage_line, line_limit.reshape(1, lines), flow_dual, step_sizes)
     return outs[0], outs[1], outs[2].reshape(rows), outs[3]
 
 

time: 42.4 us -> 27.9 us (0.66)
  local copies, waits for them, and re-layouts: 15.7 us -> 0 us
  Pallas kernels: 25.5 us -> 27.1 us
    unnamed x32 -> x0, local copies, waits for them, and re-layouts: 15.7 us -> none
    pallas_call x1 -> x2, Pallas kernels: 25.5 us -> 27.1 us  [the longest x1 24.4 us: fused(): pl.pallas_call(functools.partial(kernel, buses), out_shape=(small, jax.Sh...]
where the time goes in v2:
time: 27.9 us; the launch traced here: 27.7 us
  Pallas kernels  27.1 us (97%)
  between operations  0.64 us (2%)
    pallas_call x1, Pallas kernels, fused(): pl.pallas_call(functools.partial(kernel, buses), out_shape=(small, jax.Sh...  24.4 us
    pallas_call x1, Pallas kernels, fused(): pl.pallas_call(finish, out_shape=(small, jax.ShapeDtypeStruct(flow_dual.s...  2.72 us

profile of v2, /device:TPU:0, one launch (start us, length us, event | category | flops | bytes accessed | tf_op | source)
XLA Modules:
  0.0 27.7 jit_solution(9975713113898937683)
XLA Ops:
  0.6 24.4 %shard_map.165 = (f32[8,512]{1,0:T(8,128)}, f32[4,8,1024]{2,1,0:T(8,128)}, f32[1,8]{1,0:T(1,128)}, f32[8,512]{1,0:T(8,128)}) custom-call(f32[8]{0:T(128)} %demand_in.1, f32[8]{0:T(128)} %balance_in.1, s32[8]{0:T(128)} %start_in.1, s32[8]{0:T(128)} %outage_line_in.3, f32[4]{0:T(128)} %step_in.3, f32[8,512]{1,0:T(8,128)} %dispatch_in.1, ...), custom_call_target="tpu_custom_call" | custom-call | tf_op jit(solution)/shard_map/pallas_call | solution.py:520
  25.0 2.7 %shard_map.166 = (f32[8,512]{1,0:T(8,128)}, f32[8,8,4096]{2,1,0:T(8,128)}, f32[1,8]{1,0:T(1,128)}, f32[8,512]{1,0:T(8,128)}) custom-call(f32[8,512]{1,0:T(8,128)} %get-tuple-element.12.fresh_in, f32[4,8,1024]{2,1,0:T(8,128)} %get-tuple-element.13.base_in, f32[1,8]{1,0:T(1,128)} %get-tuple-element.14.balance_in, f32[8,512]{1,0:T(8,128)} %get-tuple-element.15.ramp_in, ...), custom_call_target="tpu_custom_call" | custom-call | tf_op jit(solution)/shard_map/pallas_call | solution.py:580

commit v3 on v2

--- a/solution.py
+++ b/solution.py
@@ -181,7 +181,7 @@
     ahead = lax.rem(tm + tms - 1, tms)
 
     barrier = pltpu.get_barrier_semaphore()
-    for k in (3, 2, 1):
+    for k in (2, 3, 1):
         pl.semaphore_signal(barrier, inc=1, device_id={"ctg": partner(me, k)}, device_id_type=MESH)
     for t in (after, ahead):
         pl.semaphore_signal(barrier, inc=1, device_id={"tm": t}, device_id_type=MESH)
@@ -275,7 +275,7 @@
 
     pl.semaphore_wait(barrier, 5)
     first = {}
-    for k in (3, 2, 1):
+    for k in (2, 3, 1):
         first[k] = to_partner(0, k, adjoint.at[:, span(partner(me, k), mine_lines)], adjoint_got.at[k - 1])
         first[k].start()
     loads[2].wait()
@@ -328,7 +328,7 @@
     extended = 2.0 * fresh - dispatch[...]
     extended_all[me] = extended
     third = {}
-    for k in (3, 2, 1):
+    for k in (2, 3, 1):
         third[k] = to_partner(2, k, extended_all.at[me], extended_all.at[me])
         third[k].start()
     last_out[...] = extended[rows - 1 :]
@@ -340,7 +340,6 @@
     stores = [pltpu.make_async_copy(new_dispatch, dispatch_to, store_sem.at[0])]
     stores[0].start()
 
-    total = jnp.sum(extended, 1, keepdims=True)
     base = None
     for k in (0, 1, 2, 3):
         if k:
@@ -348,16 +347,21 @@
         owner = partner(me, k) if k else me
         block = extended_all[owner]
         there = span(owner, mine_buses)
-        if k:
-            total = total + jnp.sum(block, 1, keepdims=True)
-        part = times(block, high[:, there], low[:, there], 1)
-        base = part if base is None else base + part
-    base_all[me] = base
+        if k < 3:
+            part = times(block, high[:, there], low[:, there], 1)
+            base = part if base is None else base + part
+    half = mine_lines // 2
     fourth = {}
-    for k in (3, 2, 1):
-        fourth[k] = to_partner(3, k, base_all.at[me], base_all.at[me])
-        fourth[k].start()
-
+    for h in range(2):
+        cut = pl.ds(h * half, half)
+        part = times(block, high[cut, there], low[cut, there], 1)
+        base_all[me, :, cut] = base[:, h * half : (h + 1) * half] + part
+        for k in (2, 3, 1):
+            piece_of = base_all.at[me, :, cut]
+            fourth[h, k] = to_partner(3 + h, k, piece_of, piece_of)
+            fourth[h, k].start()
+
+    total = jnp.sum(extended_all[0] + extended_all[1] + extended_all[2] + extended_all[3], 1, keepdims=True)
     wanted = column_of(demand, rows, f32)
     settled = balance + balance_step * (total - wanted)
     eye = lax.broadcasted_iota(jnp.int32, (rows, rows), 0) == lax.broadcasted_iota(jnp.int32, (rows, rows), 1)
@@ -375,14 +379,15 @@
 
     for k in (0, 1, 2, 3):
         if k:
-            fourth[k].wait_recv()
+            fourth[0, k].wait_recv()
+            fourth[1, k].wait_recv()
         owner = partner(me, k) if k else me
         stores.append(pltpu.make_async_copy(base_all.at[owner], base_to.at[owner], store_sem.at[3 + k]))
         stores[-1].start()
 
     for group in (first, second, third, fourth):
-        for k in (1, 2, 3):
-            group[k].wait_send()
+        for copy in group.values():
+            copy.wait_send()
     row_copy.wait_send()
     last_copy.wait_send()
     for store in stores:
@@ -554,8 +559,8 @@
             pltpu.SemaphoreType.DMA((12,)),
             pltpu.SemaphoreType.DMA((7,)),
             pltpu.SemaphoreType.DMA((8,)),
-            pltpu.SemaphoreType.DMA((4, 3)),
-            pltpu.SemaphoreType.DMA((4, 3)),
+            pltpu.SemaphoreType.DMA((5, 3)),
+            pltpu.SemaphoreType.DMA((5, 3)),
             pltpu.SemaphoreType.DMA((2,)),
             pltpu.SemaphoreType.DMA((2,)),
         ],
@@ -605,7 +610,7 @@
 def choose(*blocks):
     rows, own = blocks[0].shape
     lines = blocks[9].shape[1]
-    whole = rows == 8 and own % LANES == 0 and lines % (4 * LANES) == 0
+    whole = rows == 8 and own % LANES == 0 and lines % (8 * LANES) == 0
     if lax.axis_size("ctg") == 4 and lax.axis_size("tm") > 2 and whole:
         return fused(*blocks)
     return local(*blocks)

time: 27.9 us -> 27.3 us (0.978)
  Pallas kernels: 27.1 us -> 26.5 us
    pallas_call x1, Pallas kernels: 24.4 us -> 23.8 us  [fused(): pl.pallas_call(functools.partial(kernel, buses), out_shape=(small, jax.Sh...]
where the time goes in v3:
time: 27.3 us; the launch traced here: 27.2 us
  Pallas kernels  26.5 us (97%)
  between operations  0.64 us (2%)
    pallas_call x1, Pallas kernels, fused(): pl.pallas_call(functools.partial(kernel, buses), out_shape=(small, jax.Sh...  23.8 us
    pallas_call x1, Pallas kernels, fused(): pl.pallas_call(finish, out_shape=(small, jax.ShapeDtypeStruct(flow_dual.s...  2.72 us

profile of v3, /device:TPU:0, one launch (start us, length us, event | category | flops | bytes accessed | tf_op | source)
XLA Modules:
  0.0 27.2 jit_solution(2377691513226019493)
XLA Ops:
  0.6 23.8 %shard_map.165 = (f32[8,512]{1,0:T(8,128)}, f32[4,8,1024]{2,1,0:T(8,128)}, f32[1,8]{1,0:T(1,128)}, f32[8,512]{1,0:T(8,128)}) custom-call(f32[8]{0:T(128)} %demand_in.1, f32[8]{0:T(128)} %balance_in.1, s32[8]{0:T(128)} %start_in.1, s32[8]{0:T(128)} %outage_line_in.3, f32[4]{0:T(128)} %step_in.3, f32[8,512]{1,0:T(8,128)} %dispatch_in.1, ...), custom_call_target="tpu_custom_call" | custom-call | tf_op jit(solution)/shard_map/pallas_call | solution.py:525
  24.5 2.7 %shard_map.166 = (f32[8,512]{1,0:T(8,128)}, f32[8,8,4096]{2,1,0:T(8,128)}, f32[1,8]{1,0:T(1,128)}, f32[8,512]{1,0:T(8,128)}) custom-call(f32[8,512]{1,0:T(8,128)} %get-tuple-element.12.fresh_in, f32[4,8,1024]{2,1,0:T(8,128)} %get-tuple-element.13.base_in, f32[1,8]{1,0:T(1,128)} %get-tuple-element.14.balance_in, f32[8,512]{1,0:T(8,128)} %get-tuple-element.15.ramp_in, ...), custom_call_target="tpu_custom_call" | custom-call | tf_op jit(solution)/shard_map/pallas_call | solution.py:585
